TPU v7x, 512 devices: a whole 4x8x8 slice. The times are simulated.
512 devices in a mesh: layer: 16 (over y, core), grid: 32 (over x, z).
Axes of the slice: x: 4, y: 8, z: 8, core: 2. Of those that a mesh axis runs over, the one named last changes fastest.
Arguments:
- l_panels: bfloat16 [16, 2, 8192, 512], P('layer', None, 'grid'), may hold values from -6 to 6
- u_panels: bfloat16 [16, 2, 512, 2048], P('layer', None, 'grid'), may hold values from -0.046875 to 0.046875
- panel_fill: int32 [16, 2, 64, 4], P('layer', None, 'grid'), may hold values 0 or 1
- copy_fill: int32 [16, 64, 16], P('layer', 'grid'), may hold values 0 or 1
- sep_panels: bfloat16 [15, 8192, 256], P(None, 'grid'), may hold values from -0.25 to 0.25
- sep_owner: int32 [15], replicated, may hold values from 0 to 31
Outputs:
- schur: float32 [8192, 2048], P('grid', 'layer')
All inputs are finite; a program needn't handle non-finite values. No bound on the sum of `panel_fill` or of `copy_fill` on one device may be relied on, other than what follows from the above.
Results may differ from a plain program's by a relative error of at most 0.0035.
Values may be sent and summed in bfloat16 or wider, within the bound.
A program may use at most 64 MiB of HBM per device.

v0:
```python
import jax
import jax.numpy as jnp
from jax import lax
from jax.sharding import PartitionSpec as P

BLOCK = 128


def from_partner(x, axis, apart):
    return lax.ppermute(x, axis, [(i, i ^ 1 << apart) for i in range(lax.axis_size(axis))])


def spread(x, axis, root):
    mine = lax.axis_index(axis) == root
    return lax.psum(jnp.where(mine, x, jnp.zeros_like(x)), axis)


def local(l_panels, u_panels, panel_fill, copy_fill, sep_panels, sep_owner):
    panel_count = l_panels.shape[1]
    row_count = l_panels.shape[2]
    panel_width = l_panels.shape[3]
    columns = u_panels.shape[3]
    fill_panel = panel_fill[0].astype(jnp.bfloat16)
    masked = (
        l_panels[0].reshape(panel_count, row_count // BLOCK, BLOCK, panel_width // BLOCK, BLOCK)
        * fill_panel[:, :, None, :, None]
    ).reshape(panel_count, row_count, panel_width)
    running = jnp.zeros((row_count, columns), jnp.float32)
    piece = lax.all_gather(u_panels, "grid", axis=2, tiled=True)
    for k in range(panel_count):
        column_part = masked[k]
        running = running + jnp.dot(column_part, piece[0, k], preferred_element_type=jnp.float32)
    fill_copy = copy_fill[0].astype(jnp.float32)
    layer_copy = -(
        running.reshape(row_count // BLOCK, BLOCK, columns // BLOCK, BLOCK)
        * fill_copy[:, None, :, None]
    ).reshape(row_count, columns)
    layers = lax.axis_size("layer")
    level_count = layers.bit_length() - 1
    layer_index = lax.axis_index("layer")
    column_width = columns // layers
    combined = layer_copy
    for level_index in range(level_count):
        partner = from_partner(combined, "layer", level_index)
        combined = combined + partner
        node_index = layers - (layers >> level_index) + (layer_index >> level_index + 1)
        owner_index = sep_owner[node_index]
        pivot_rows = spread(combined.astype(jnp.bfloat16), "grid", owner_index)
        factor = lax.dynamic_index_in_dim(sep_panels, node_index, 0, keepdims=False)
        combined = combined - jnp.dot(factor, pivot_rows, preferred_element_type=jnp.float32)
    return lax.dynamic_slice_in_dim(combined, layer_index * column_width, column_width, 1)


def solution(mesh):
    return jax.shard_map(
        local,
        mesh=mesh,
        in_specs=(
            P("layer", None, "grid", None),
            P("layer", None, "grid", None),
            P("layer", None, "grid", None),
            P("layer", "grid", None),
            P(None, "grid", None),
            P(),
        ),
        out_specs=P("grid", "layer"),
        check_vma=False,
    )
```

profile of v0, /device:TPU:56, one launch (start us, length us, event | category | flops | bytes accessed | tf_op | source)
XLA Modules:
  0.0 1016.0 jit_solution(16947582631460522231)
XLA Ops:
  6.5 0.0 copy-start
  6.5 0.0 all-gather.2.cloned.1.call-start
  6.5 0.7 all-gather.2.cloned.1.call-update
  7.3 0.0 all-reduce.5.cloned.1.call-start
  7.3 1.2 reshape_squeeze.3
  8.5 0.7 convert_bitcast_fusion
  9.2 0.7 convert_bitcast_fusion.1
  9.8 0.3 broadcast_multiply_fusion
  10.2 0.2 fusion.20
  10.3 92.7 %all-gather.2.cloned.1.call-done = bf16[1,2,512,2048]{3,2,1,0:T(8,128)(2,1)} async-done(((bf16[1,2,16,2048]{3,2,1,0:T(8,128)(2,1)}), bf16[1,2,512,2048]{3,2,1,0:T(8,128)(2,1)}) %all-gather.2.cloned.1.call-update) | async-done | bytes 4194320 | tf_op jit(solution)/shard_map/all_gather | solution.py:29
  103.1 0.0 copy-start.1
  103.1 2.4 fusion.2
  105.5 0.2 mul.24
  105.7 0.2 copy-done.1
  105.9 0.0 copy-start.2
  105.9 2.5 fusion.1
  108.4 1.9 collective-permute-start
  110.4 0.0 copy-done.2
  110.4 0.7 fusion.21
  111.7 3.1 collective-permute-done
  114.8 4.4 convert_select_fusion.3
  119.2 0.0 all-reduce.5.cloned.1.call-update
  119.3 0.0 all-reduce.7.cloned.1.call-start
  119.3 157.3 %all-reduce.5.cloned.1.call-done = bf16[256,2048]{1,0:T(8,128)(2,1)} async-done(((bf16[256,2048]{1,0:T(8,128)(2,1)}), bf16[256,2048]{1,0:T(8,128)(2,1)}) %all-reduce.5.cloned.1.call-update) | async-done | bytes 1048592 | tf_op jit(solution)/shard_map/psum | solution.py:15
  276.6 0.0 copy-done
  276.6 3.7 convolution_subtract_fusion.2
  280.3 3.3 collective-permute-start.1
  284.3 41.0 %collective-permute-done.1 = f32[256,2048]{1,0:T(8,128)} collective-permute-done((f32[256,2048]{1,0:T(8,128)}, f32[256,2048]{1,0:T(8,128)}, u32[]{:S(2)}, u32[]{:S(2)}) %collective-permute-start.1) | collective-permute-done | bytes 2097184 | tf_op jit(solution)/shard_map/ppermute | solution.py:10
  325.3 4.4 convert_select_fusion.2
  329.8 0.0 all-reduce.7.cloned.1.call-update
  329.8 0.0 all-reduce.9.cloned.1.call-start
  329.8 158.1 %all-reduce.7.cloned.1.call-done = bf16[256,2048]{1,0:T(8,128)(2,1)} async-done(((bf16[256,2048]{1,0:T(8,128)(2,1)}), bf16[256,2048]{1,0:T(8,128)(2,1)}) %all-reduce.7.cloned.1.call-update) | async-done | bytes 1048592 | tf_op jit(solution)/shard_map/psum | solution.py:15
  487.9 3.7 convolution_subtract_fusion.1
  491.6 4.2 collective-permute-start.2
  496.4 86.1 %collective-permute-done.2 = f32[256,2048]{1,0:T(8,128)} collective-permute-done((f32[256,2048]{1,0:T(8,128)}, f32[256,2048]{1,0:T(8,128)}, u32[]{:S(2)}, u32[]{:S(2)}) %collective-permute-start.2) | collective-permute-done | bytes 2097184 | tf_op jit(solution)/shard_map/ppermute | solution.py:10
  582.5 4.4 convert_select_fusion.1
  586.9 0.0 all-reduce.9.cloned.1.call-update
  586.9 0.0 all-reduce.11.cloned.1.call-start
  587.0 158.1 %all-reduce.9.cloned.1.call-done = bf16[256,2048]{1,0:T(8,128)(2,1)} async-done(((bf16[256,2048]{1,0:T(8,128)(2,1)}), bf16[256,2048]{1,0:T(8,128)(2,1)}) %all-reduce.9.cloned.1.call-update) | async-done | bytes 1048592 | tf_op jit(solution)/shard_map/psum | solution.py:15
  745.1 3.7 convolution_subtract_fusion
  748.8 5.1 collective-permute-start.3
  754.5 80.9 %collective-permute-done.3 = f32[256,2048]{1,0:T(8,128)} collective-permute-done((f32[256,2048]{1,0:T(8,128)}, f32[256,2048]{1,0:T(8,128)}, u32[]{:S(2)}, u32[]{:S(2)}) %collective-permute-start.3) | collective-permute-done | bytes 2097184 | tf_op jit(solution)/shard_map/ppermute | solution.py:10
  835.4 4.4 convert_select_fusion
  839.9 0.0 all-reduce.11.cloned.1.call-update
  839.9 166.3 %all-reduce.11.cloned.1.call-done = bf16[256,2048]{1,0:T(8,128)(2,1)} async-done(((bf16[256,2048]{1,0:T(8,128)(2,1)}), bf16[256,2048]{1,0:T(8,128)(2,1)}) %all-reduce.11.cloned.1.call-update) | async-done | bytes 1048592 | tf_op jit(solution)/shard_map/psum | solution.py:15
  1006.2 1.7 fusion.7
  1007.8 1.6 dynamic-slice_subtract_fusion
Async XLA Ops:
  6.5 270.1 %copy-start = (bf16[15,256,256]{2,1,0:T(8,128)(2,1)S(1)}, bf16[15,256,256]{2,1,0:T(8,128)(2,1)}, u32[]{:S(2)}) copy-start(bf16[15,256,256]{2,1,0:T(8,128)(2,1)} %param.10) | copy-start | bytes 5898244
  6.5 96.5 %all-gather.2.cloned.1.call-start = ((), (), s32[]{:S(2)}) async-start(), calls=%async_computation | async-start | bytes 4325376 | tf_op jit(solution)/shard_map/all_gather | solution.py:29
  7.3 269.4 %all-reduce.5.cloned.1.call-start = ((), (), s32[]{:S(2)}) async-start(), calls=%async_computation.1 | async-start | bytes 2097152 | tf_op jit(solution)/shard_map/psum | solution.py:15
  103.1 2.8 copy-start.1
  105.9 4.5 copy-start.2
  108.4 6.4 collective-permute-start
  119.3 368.7 %all-reduce.7.cloned.1.call-start = ((), (), s32[]{:S(2)}) async-start(), calls=%async_computation.2 | async-start | bytes 2097152 | tf_op jit(solution)/shard_map/psum | solution.py:15
  280.3 45.0 %collective-permute-start.1 = (f32[256,2048]{1,0:T(8,128)}, f32[256,2048]{1,0:T(8,128)}, u32[]{:S(2)}, u32[]{:S(2)}) collective-permute-start(f32[256,2048]{1,0:T(8,128)} %convolution_subtract_fusion.2), channel_id=1, source_target_pairs={{0,64},{32,96},{64,0},{96,32},{128,192},{160,224},{192,128},{224,1... | collective-permute-start | bytes 6291464 | tf_op jit(solution)/shard_map/ppermute | solution.py:10
  329.8 415.3 %all-reduce.9.cloned.1.call-start = ((), (), s32[]{:S(2)}) async-start(), calls=%async_computation.3 | async-start | bytes 2097152 | tf_op jit(solution)/shard_map/psum | solution.py:15
  491.6 90.9 %collective-permute-start.2 = (f32[256,2048]{1,0:T(8,128)}, f32[256,2048]{1,0:T(8,128)}, u32[]{:S(2)}, u32[]{:S(2)}) collective-permute-start(f32[256,2048]{1,0:T(8,128)} %convolution_subtract_fusion.1), channel_id=1, source_target_pairs={{0,128},{32,160},{64,192},{96,224},{128,0},{160,32},{192,64},{224,... | collective-permute-start | bytes 6291464 | tf_op jit(solution)/shard_map/ppermute | solution.py:10
  586.9 419.2 %all-reduce.11.cloned.1.call-start = ((), (), s32[]{:S(2)}) async-start(), calls=%async_computation.4 | async-start | bytes 2097152 | tf_op jit(solution)/shard_map/psum | solution.py:15
  748.8 86.6 %collective-permute-start.3 = (f32[256,2048]{1,0:T(8,128)}, f32[256,2048]{1,0:T(8,128)}, u32[]{:S(2)}, u32[]{:S(2)}) collective-permute-start(f32[256,2048]{1,0:T(8,128)} %convolution_subtract_fusion), channel_id=1, source_target_pairs={{0,256},{32,288},{64,320},{96,352},{128,384},{160,416},{192,448},{... | collective-permute-start | bytes 6291464 | tf_op jit(solution)/shard_map/ppermute | solution.py:10
Sparse Core Ops, SparseCore 0:
  10.5 92.5 all-gather.1
  119.4 157.1 all-reduce.4
  329.9 157.9 all-reduce.6
  587.0 158.0 all-reduce.8
  840.0 166.1 all-reduce.10
where the time goes:
time: 1020 us
  waiting for transfers between devices  944 us (93%)
  other arithmetic  21 us (2%)
  matrix products  17.7 us (2%)
  between operations  15.7 us (2%)
  starting transfers between devices  14.7 us (1%)
    psum x4, waiting for transfers between devices, spread(): return lax.psum(jnp.where(mine, x, jnp.zeros_like(x)), axis)  640 us
    ppermute x4, waiting for transfers between devices, from_partner(): lax.ppermute(x, axis, [(i, i ^ 1 << apart) for i in range(lax.axis_size(a...  211 us
    all_gather x1, waiting for transfers between devices, local(): piece = lax.all_gather(u_panels, 'grid', axis=2, tiled=True)  92.7 us
  transfers between devices with their start and end apart: 9, of which 9 were waited for; matrix products, arithmetic and copies ran while one was open for 0% of the time, Pallas kernels for 0%

commit v1 on v0

--- a/solution.py
+++ b/solution.py
@@ -15,11 +15,24 @@
     return lax.psum(jnp.where(mine, x, jnp.zeros_like(x)), axis)
 
 
+def reorder(x, count):
+    bits = count.bit_length() - 1
+    lead = x.ndim - 1
+    split = x.reshape(*x.shape[:-1], *(2,) * bits, x.shape[-1] // count)
+    axes = [*range(lead), *reversed(range(lead, lead + bits)), lead + bits]
+    return split.transpose(axes).reshape(x.shape)
+
+
 def local(l_panels, u_panels, panel_fill, copy_fill, sep_panels, sep_owner):
     panel_count = l_panels.shape[1]
     row_count = l_panels.shape[2]
     panel_width = l_panels.shape[3]
     columns = u_panels.shape[3]
+    layers = lax.axis_size("layer")
+    level_count = layers.bit_length() - 1
+    layer_index = lax.axis_index("layer")
+    u_panels = reorder(u_panels, layers)
+    copy_fill = reorder(copy_fill, layers)
     fill_panel = panel_fill[0].astype(jnp.bfloat16)
     masked = (
         l_panels[0].reshape(panel_count, row_count // BLOCK, BLOCK, panel_width // BLOCK, BLOCK)
@@ -35,20 +48,20 @@
         running.reshape(row_count // BLOCK, BLOCK, columns // BLOCK, BLOCK)
         * fill_copy[:, None, :, None]
     ).reshape(row_count, columns)
-    layers = lax.axis_size("layer")
-    level_count = layers.bit_length() - 1
-    layer_index = lax.axis_index("layer")
-    column_width = columns // layers
     combined = layer_copy
     for level_index in range(level_count):
-        partner = from_partner(combined, "layer", level_index)
-        combined = combined + partner
+        half = combined.shape[1] // 2
+        bit = layer_index >> level_index & 1
+        keep = lax.dynamic_slice_in_dim(combined, bit * half, half, 1)
+        give = lax.dynamic_slice_in_dim(combined, (1 - bit) * half, half, 1)
+        wire = jnp.float32 if level_index < 2 else jnp.bfloat16
+        combined = keep + from_partner(give.astype(wire), "layer", level_index).astype(jnp.float32)
         node_index = layers - (layers >> level_index) + (layer_index >> level_index + 1)
         owner_index = sep_owner[node_index]
         pivot_rows = spread(combined.astype(jnp.bfloat16), "grid", owner_index)
         factor = lax.dynamic_index_in_dim(sep_panels, node_index, 0, keepdims=False)
         combined = combined - jnp.dot(factor, pivot_rows, preferred_element_type=jnp.float32)
-    return lax.dynamic_slice_in_dim(combined, layer_index * column_width, column_width, 1)
+    return combined
 
 
 def solution(mesh):

time: 1020 us -> 770 us (0.75)
  waiting for transfers between devices: 944 us -> 714 us
  other arithmetic: 21 us -> 6.53 us
    ppermute x4, waiting for transfers between devices: 211 us -> 17.6 us  [from_partner(): lax.ppermute(x, axis, [(i, i ^ 1 << apart) for i in range(lax.axis_size(a...]
    psum x4, waiting for transfers between devices: 640 us -> 605 us  [spread(): return lax.psum(jnp.where(mine, x, jnp.zeros_like(x)), axis)]
    select_n x4, other arithmetic: 17.7 us -> 4.85 us  [spread(): return lax.psum(jnp.where(mine, x, jnp.zeros_like(x)), axis)]
  transfers between devices with their start and end apart: 9 -> 9, of which waited for: 9 -> 9; matrix products, arithmetic and copies ran while one was open for 0% -> 1% of each run, Pallas kernels for 0% -> 0%
where the time goes in v1:
time: 770 us; the launch traced here: 769 us
  waiting for transfers between devices  714 us (93%)
  between operations  15.8 us (2%)
  starting transfers between devices  14.7 us (2%)
  matrix products  9.78 us (1%)
  local copies, waits for them, and re-layouts  7.93 us (1%)
    psum x4, waiting for transfers between devices, spread(): return lax.psum(jnp.where(mine, x, jnp.zeros_like(x)), axis)  605 us
    all_gather x1, waiting for transfers between devices, local(): piece = lax.all_gather(u_panels, 'grid', axis=2, tiled=True)  91.1 us
    ppermute x4, waiting for transfers between devices, from_partner(): lax.ppermute(x, axis, [(i, i ^ 1 << apart) for i in range(lax.axis_size(a...  17.6 us
  transfers between devices with their start and end apart: 9, of which 9 were waited for; matrix products, arithmetic and copies ran while one was open for 1% of the time, Pallas kernels for 0%

profile of v1, /device:TPU:56, one launch (start us, length us, event | category | flops | bytes accessed | tf_op | source)
XLA Modules:
  0.0 768.9 jit_solution(11261372993975897174)
XLA Ops:
  6.5 0.0 copy-start
  6.5 0.0 all-gather.2.cloned.1.call-start
  6.5 1.1 reshape.28
  7.7 0.1 copy.23
  7.8 0.7 reshape.29
  8.5 0.0 all-gather.2.cloned.1.call-update
  8.5 0.0 all-reduce.5.cloned.1.call-start
  8.6 1.2 reshape_squeeze.3
  9.8 0.7 convert_element_type.52
  10.4 0.1 convert_element_type.53
  10.5 0.1 copy.9
  10.7 0.1 convert_element_type.55
  10.8 0.7 convert_bitcast_fusion
  11.4 0.3 broadcast_multiply_fusion
  11.8 0.2 fusion.23
  11.9 91.1 %all-gather.2.cloned.1.call-done = bf16[1,2,512,2048]{3,2,1,0:T(8,128)(2,1)} async-done(((bf16[1,2,16,2048]{3,2,1,0:T(8,128)(2,1)}), bf16[1,2,512,2048]{3,2,1,0:T(8,128)(2,1)}) %all-gather.2.cloned.1.call-update) | async-done | bytes 4194320 | tf_op jit(solution)/shard_map/all_gather | solution.py:42
  103.1 0.0 copy-start.3
  103.1 2.4 fusion.2
  105.5 0.2 mul.45
  105.7 0.2 copy-done.3
  105.9 1.2 fusion.1
  107.1 0.0 copy-start.1
  107.2 1.3 copy-done.1
  108.5 0.0 copy-start.5
  108.5 1.0 constant_dynamic-slice_fusion.1
  109.5 1.9 collective-permute-start
  111.5 0.0 copy-done.5
  111.5 0.7 fusion.24
  112.7 1.6 collective-permute-done
  114.3 0.0 copy-start.2
  114.3 2.6 convert_select_fusion
  116.9 0.0 all-reduce.5.cloned.1.call-update
  116.9 0.0 all-reduce.7.cloned.1.call-start
  116.9 0.0 copy-done.2
  116.9 155.4 %all-reduce.5.cloned.1.call-done = bf16[256,1024]{1,0:T(8,128)(2,1)} async-done(((bf16[256,1024]{1,0:T(8,128)(2,1)}), bf16[256,1024]{1,0:T(8,128)(2,1)}) %all-reduce.5.cloned.1.call-update) | async-done | bytes 524304 | tf_op jit(solution)/shard_map/psum | solution.py:15
  272.3 0.0 copy-done
  272.3 2.0 convolution_subtract_fusion
  274.3 0.8 constant_dynamic-slice_fusion
  275.2 3.3 collective-permute-start.1
  279.2 7.3 collective-permute-done.1
  286.5 0.0 copy-start.4
  286.5 0.9 convert_select_fusion.1
  287.4 0.0 all-reduce.7.cloned.1.call-update
  287.4 0.0 all-reduce.9.cloned.1.call-start
  287.5 0.0 copy-done.4
  287.5 152.3 %all-reduce.7.cloned.1.call-done = bf16[256,512]{1,0:T(8,128)(2,1)} async-done(((bf16[256,512]{1,0:T(8,128)(2,1)}), bf16[256,512]{1,0:T(8,128)(2,1)}) %all-reduce.7.cloned.1.call-update) | async-done | bytes 262160 | tf_op jit(solution)/shard_map/psum | solution.py:15
  439.8 1.3 convolution_subtract_fusion.1
  441.2 4.2 collective-permute-start.2
  446.1 4.2 collective-permute-done.2
  450.3 0.7 fusion.8
  451.0 0.0 all-reduce.9.cloned.1.call-update
  451.1 0.0 all-reduce.11.cloned.1.call-start
  451.1 148.7 %all-reduce.9.cloned.1.call-done = bf16[256,256]{1,0:T(8,128)(2,1)} async-done(((bf16[256,256]{1,0:T(8,128)(2,1)}), bf16[256,256]{1,0:T(8,128)(2,1)}) %all-reduce.9.cloned.1.call-update) | async-done | bytes 131088 | tf_op jit(solution)/shard_map/psum | solution.py:15
  599.9 1.1 convolution_subtract_fusion.2
  601.0 5.1 collective-permute-start.3
  606.6 4.5 collective-permute-done.3
  611.2 0.7 fusion.18
  611.8 0.0 all-reduce.11.cloned.1.call-update
  611.8 148.8 %all-reduce.11.cloned.1.call-done = bf16[256,128]{1,0:T(8,128)(2,1)} async-done(((bf16[256,128]{1,0:T(8,128)(2,1)}), bf16[256,128]{1,0:T(8,128)(2,1)}) %all-reduce.11.cloned.1.call-update) | async-done | bytes 65552 | tf_op jit(solution)/shard_map/psum | solution.py:15
  760.7 1.7 convolution_subtract_fusion.3
  (2 shorter events, 0.0 us)
Async XLA Ops:
  6.5 265.8 %copy-start = (bf16[15,256,256]{2,1,0:T(8,128)(2,1)S(1)}, bf16[15,256,256]{2,1,0:T(8,128)(2,1)}, u32[]{:S(2)}) copy-start(bf16[15,256,256]{2,1,0:T(8,128)(2,1)} %param.10) | copy-start | bytes 5898244
  6.5 96.5 %all-gather.2.cloned.1.call-start = ((), (), s32[]{:S(2)}) async-start(), calls=%async_computation | async-start | bytes 4325376 | tf_op jit(solution)/shard_map/all_gather | solution.py:42
  8.5 263.8 %all-reduce.5.cloned.1.call-start = ((), (), s32[]{:S(2)}) async-start(), calls=%async_computation.1 | async-start | bytes 1048576 | tf_op jit(solution)/shard_map/psum | solution.py:15
  103.1 2.8 copy-start.3
  107.1 1.3 copy-start.1
  108.5 3.0 copy-start.5
  109.5 4.8 collective-permute-start
  114.3 2.7 copy-start.2
  116.9 322.9 %all-reduce.7.cloned.1.call-start = ((), (), s32[]{:S(2)}) async-start(), calls=%async_computation.2 | async-start | bytes 524288 | tf_op jit(solution)/shard_map/psum | solution.py:15
  275.2 11.3 %collective-permute-start.1 = (f32[256,512]{1,0:T(8,128)}, f32[256,512]{1,0:T(8,128)S(1)}, u32[]{:S(2)}, u32[]{:S(2)}) collective-permute-start(f32[256,512]{1,0:T(8,128)} %constant_dynamic-slice_fusion), channel_id=1, source_target_pairs={{0,64},{32,96},{64,0},{96,32},{128,192},{160,224},{192,128},{224,1... | collective-permute-start | bytes 1572872 | tf_op jit(solution)/shard_map/ppermute | solution.py:10
  286.5 1.0 copy-start.4
  287.4 312.4 %all-reduce.9.cloned.1.call-start = ((), (), s32[]{:S(2)}) async-start(), calls=%async_computation.3 | async-start | bytes 262144 | tf_op jit(solution)/shard_map/psum | solution.py:15
  441.2 9.2 %collective-permute-start.2 = (bf16[256,256]{1,0:T(8,128)(2,1)S(1)}, bf16[256,256]{1,0:T(8,128)(2,1)S(1)}, u32[]{:S(2)}, u32[]{:S(2)}) collective-permute-start(bf16[256,256]{1,0:T(8,128)(2,1)S(1)} %dynamic-slice_convert_fusion), channel_id=1, source_target_pairs={{0,128},{32,160},{64,192},{96,224},{128,0},{160,32},{192,64},{224,... | collective-permute-start | bytes 393224 | tf_op jit(solution)/shard_map/ppermute | solution.py:10
  451.1 309.6 %all-reduce.11.cloned.1.call-start = ((), (), s32[]{:S(2)}) async-start(), calls=%async_computation.4 | async-start | bytes 131072 | tf_op jit(solution)/shard_map/psum | solution.py:15
  601.0 10.2 %collective-permute-start.3 = (bf16[256,128]{1,0:T(8,128)(2,1)S(1)}, bf16[256,128]{1,0:T(8,128)(2,1)S(1)}, u32[]{:S(2)}, u32[]{:S(2)}) collective-permute-start(bf16[256,128]{1,0:T(8,128)(2,1)S(1)} %dynamic-slice_convert_fusion.1), channel_id=1, source_target_pairs={{0,256},{32,288},{64,320},{96,352},{128,384},{160,416},{192,448},{... | collective-permute-start | bytes 196616 | tf_op jit(solution)/shard_map/ppermute | solution.py:10
Sparse Core Ops, SparseCore 0:
  10.5 92.5 all-gather.1
  117.0 155.2 all-reduce.4
  287.5 152.1 all-reduce.6
  451.2 148.6 all-reduce.8
  612.0 148.6 all-reduce.10

commit v2 on v0

v2 whole, which is shorter than its diff:
```python
import jax
import jax.numpy as jnp
from jax import lax
from jax.experimental import pallas as pl
from jax.experimental.pallas import tpu as pltpu
from jax.sharding import PartitionSpec as P

BLOCK = 128
X = 4
Z = 8
GROUP = BLOCK // X
LEVELS = 4
F32 = jnp.float32
BF16 = jnp.bfloat16


def turned(v, groups):
    shift = groups % X * GROUP
    return pltpu.roll(v, shift, 1) if shift else v


def by_group(pieces):
    group = lax.broadcasted_iota(jnp.int32, pieces[0].shape, 1) // GROUP
    out = pieces[0]
    for g in range(1, X):
        out = jnp.where(group == g, pieces[g], out)
    return out


def by_half(low, high):
    lane = lax.broadcasted_iota(jnp.int32, low.shape, 1)
    return jnp.where(lane < BLOCK // 2, low, high)


def column_block(tile, group):
    return (tile >> 1) + 2 * (tile & 1) + 4 * (group >> 1) + 8 * (group & 1)


def dot(a, b):
    return jnp.dot(a, b, preferred_element_type=F32)


def kernel(
    owner_ref, panel_fill_ref, copy_fill_ref, l_ref, u_ref, sep_ref, out_ref,
    u_row, u_buf, l_buf, mask, acc, other, half, sep_buf,
    give1, take1, state1, pack2, give2, take2, state2, pack3, give3, take3, state3,
    cand0, parts0, pivot0, cand1, parts1, pivot1, slices, final,
    u_sem, mask_sem, l_sem, ring_sem, core_sem, sep_sem, own_sem, y_sem, part_sem, pivot_sem, final_sem,
):
    layer = lax.axis_index("layer")
    grid = lax.axis_index("grid")
    x = grid // Z
    z = grid % Z
    rows = l_ref.shape[2]
    width = l_ref.shape[3]
    panels = l_ref.shape[1]
    depth = u_ref.shape[2]

    def along_x(d):
        return (x + d) % X

    def along_z(d):
        return (z + d) % Z

    def bit(level):
        return layer // 2**level % 2

    def partner(level):
        return layer + 2**level * (1 - 2 * bit(level))

    def remote(src, dst, sems, index, device):
        return pltpu.make_async_remote_copy(
            src_ref=src,
            dst_ref=dst,
            send_sem=sems.at[(0, *index)],
            recv_sem=sems.at[(1, *index)],
            device_id=device,
            device_id_type=pl.DeviceIdType.MESH,
        )

    def to_x(d):
        return {"grid": along_x(d) * Z + z}

    def to_z(d):
        return {"grid": x * Z + along_z(d)}

    barrier = pltpu.get_barrier_semaphore()
    peers = [to_x(d) for d in range(1, X)] + [to_z(d) for d in range(1, Z)]
    peers += [{"layer": partner(level)} for level in range(LEVELS)]
    for peer in peers:
        pl.semaphore_signal(barrier, inc=1, device_id=peer, device_id_type=pl.DeviceIdType.MESH)

    own_sep = []
    for level in range(LEVELS):
        node = 2**LEVELS - (2**LEVELS >> level) + layer // 2 ** (level + 1)
        own_sep.append(pltpu.make_async_copy(sep_ref.at[node], sep_buf.at[level, x], own_sem.at[level]))
        own_sep[level].start()

    turns = {}
    for tile in range(X):
        for group in range(X):
            block = column_block(tile, group)
            piece = u_ref[0, :, :, block * BLOCK : (block + 1) * BLOCK].astype(F32).reshape(panels * depth, BLOCK)
            turns[tile, group] = [turned(piece, n) for n in range(X)]
        for quarter in range(X):
            mixed = by_group([turns[tile, group][(group - quarter) % X] for group in range(X)])
            u_row[quarter, :, :, tile * BLOCK : (tile + 1) * BLOCK] = mixed.astype(BF16).reshape(panels, depth, BLOCK)
    u_buf[:, x, z] = u_row[x]

    pl.semaphore_wait(barrier, len(peers))

    u_copies = []
    for d in range(1, X):
        u_copies.append(remote(u_row.at[along_x(d)], u_buf.at[:, x, z], u_sem, (d - 1,), to_x(d)))
        u_copies[-1].start()

    for k in range(panels):
        for r in range(rows // BLOCK):
            for c in range(width // BLOCK):
                fill = panel_fill_ref[0, k, r, c].astype(F32)
                piece = l_ref[0, k, r * BLOCK : (r + 1) * BLOCK, c * BLOCK : (c + 1) * BLOCK].astype(F32) * fill
                l_buf[x, r * BLOCK : (r + 1) * BLOCK, k * width + c * BLOCK : k * width + (c + 1) * BLOCK] = (
                    piece.astype(BF16)
                )

    def l_copy(index, source, part, d):
        where = l_buf.at[along_x(source), pl.ds(part * BLOCK, BLOCK)]
        return remote(where, where, l_sem, (index,), to_x(d))

    l_copies = [l_copy(0, 0, 0, 1), l_copy(1, 0, 1, -1), l_copy(2, 0, 1, 1), l_copy(3, 0, 0, -1)]
    for copy in l_copies:
        copy.start()

    shape = (8, BLOCK)
    sublane = lax.broadcasted_iota(jnp.int32, shape, 0)
    for tile in range(X):
        picked = []
        for group in range(X):
            value = jnp.zeros(shape, F32)
            for r in range(rows // BLOCK):
                fill = copy_fill_ref[0, r, column_block(tile, group)].astype(F32)
                value = jnp.where(sublane == r, -fill, value)
            picked.append(value)
        mask[x, :, tile * BLOCK : (tile + 1) * BLOCK] = by_group(picked)
    mask_copies = []
    for d in range(1, X):
        mask_copies.append(remote(mask.at[x], mask.at[x], mask_sem, (d - 1,), to_x(d)))
        mask_copies[-1].start()

    for copy in u_copies:
        copy.wait_recv()

    def ring_copy(step, way):
        block = along_z(-way * (step - 1))
        if step < Z // 2:
            where = u_buf.at[:, :, block]
        else:
            where = u_buf.at[0 if way > 0 else 1, :, block]
        return remote(where, where, ring_sem, (2 * (step - 1) + (way < 0),), to_z(way))

    ring = {}
    for step in range(1, Z // 2 + 1):
        for way in (1, -1):
            if step > 1:
                ring[step - 1, way].wait_recv()
            ring[step, way] = ring_copy(step, way)
            ring[step, way].start()
        if step == 2:
            for index, (source, part, way) in enumerate(((-1, 0, 1), (1, 1, -1))):
                l_copies[index].wait_recv()
                l_copies.append(l_copy(4 + index, source, part, way))
                l_copies[-1].start()

    sep_copies = []
    for level in range(LEVELS):
        own_sep[level].wait()
        where = sep_buf.at[level, x]
        sep_copies.append([remote(where, where, sep_sem, (level, d - 1), to_x(d)) for d in range(1, X)])
        for copy in sep_copies[level]:
            copy.start()

    for copy in mask_copies:
        copy.wait_recv()
    for way in (1, -1):
        ring[Z // 2, way].wait_recv()

    def weight(level, row_block):
        node = 2**LEVELS - (2**LEVELS >> level) + layer // 2 ** (level + 1)
        return jnp.where(owner_ref[node] == row_block * Z + z, 1.0, 0.0).astype(F32)

    core_copies = []
    order = [along_x(d) for d in (0, -1, 1, 2)]
    waits = [[], [2], [3], [4, 5]]
    for index, row_block in enumerate(order):
        for which in waits[index]:
            l_copies[which].wait_recv()
        u_all = u_buf[...].reshape(panels * width, X * BLOCK)
        for r in range(rows // BLOCK):
            part = dot(l_buf[row_block, r * BLOCK : (r + 1) * BLOCK], u_all) * mask[row_block, r : r + 1]
            for h in range(2):
                acc[h, row_block, r * BLOCK : (r + 1) * BLOCK] = part[:, h * 2 * BLOCK : (h + 1) * 2 * BLOCK]
        core_copies.append(
            remote(acc.at[1 - bit(0), row_block], other.at[row_block], core_sem, (index,), {"layer": partner(0)})
        )
        core_copies[-1].start()

    def spread(level, cand, parts, pivot):
        def part_copy(d):
            return remote(cand.at[:, along_z(d)], parts.at[d], part_sem, (level, d), to_z(d))

        def pivot_copy(d):
            where = pivot.at[:, z]
            return remote(where, where, pivot_sem, (level, d), to_z(d))

        def each(act):
            def body(d, carry):
                act(d)
                return carry

            lax.fori_loop(1, Z, body, 0)

        each(lambda d: part_copy(d).start())
        total = cand[:, z].astype(F32)

        def add(d, total):
            part_copy(d).wait_recv()
            return total + parts[d].astype(F32)

        total = lax.fori_loop(1, Z, add, total)
        pivot[:, z] = total.astype(BF16)
        each(lambda d: pivot_copy(d).start())
        each(lambda d: pivot_copy(d).wait_recv())
        each(lambda d: part_copy(d).wait_send())
        each(lambda d: pivot_copy(d).wait_send())

    picked = jnp.zeros((rows, 2 * BLOCK), F32)
    for index, row_block in enumerate(order):
        core_copies[index].wait_recv()
        value = acc[bit(0), row_block] + other[row_block]
        for h in range(2):
            half[h, row_block] = value[:, h * BLOCK : (h + 1) * BLOCK]
        picked = picked + weight(0, row_block) * value
    for h in range(2):
        cand0[h] = picked[:, h * BLOCK : (h + 1) * BLOCK].astype(BF16).reshape(Z, rows // Z, BLOCK)
    spread(0, cand0, parts0, pivot0)

    for copy in sep_copies[0]:
        copy.wait_recv()
    y_copies = []
    giving = 1 - bit(1)
    for row_block in range(X):
        update = dot(sep_buf[0, row_block], pivot0[giving].reshape(rows, BLOCK))
        give1[row_block] = (half[giving, row_block] - update).astype(BF16)
        y_copies.append(
            remote(give1.at[row_block], take1.at[row_block], y_sem, (row_block,), {"layer": partner(1)})
        )
        y_copies[-1].start()
    picked = jnp.zeros((rows, BLOCK), F32)
    for row_block in range(X):
        update = dot(sep_buf[0, row_block], pivot0[bit(1)].reshape(rows, BLOCK))
        value = half[bit(1), row_block] - update
        y_copies[row_block].wait_recv()
        value = value + take1[row_block].astype(F32)
        state1[row_block] = value
        picked = picked + weight(1, row_block) * value
    cand1[0, 0] = picked.astype(BF16).reshape(Z, rows // Z, BLOCK)
    spread(1, cand1.at[0], parts1.at[0], pivot1.at[0])

    for copy in sep_copies[1]:
        copy.wait_recv()
    for pair in range(2):
        low, high = [
            state1[row_block] - dot(sep_buf[1, row_block], pivot1[0, 0].reshape(rows, BLOCK))
            for row_block in (pair, pair + 2)
        ]
        pack2[0, pair] = by_half(low, turned(high, 2))
        pack2[1, pair] = by_half(turned(low, 2), high)
    give2[...] = pack2[1 - bit(2)].astype(BF16)
    y_copies.append(remote(give2, take2, y_sem, (X,), {"layer": partner(2)}))
    y_copies[-1].start()
    y_copies[-1].wait_recv()
    value = pack2[bit(2)] + take2[...].astype(F32)
    state2[...] = value
    picked = by_half(*[weight(2, 2 * h) * value[0] + weight(2, 2 * h + 1) * value[1] for h in range(2)])
    picked = picked + turned(picked, 2)
    cand1[1, 0] = picked.astype(BF16).reshape(Z, rows // Z, BLOCK)
    spread(2, cand1.at[1], parts1.at[1], pivot1.at[1])

    for copy in sep_copies[2]:
        copy.wait_recv()
    updates = [dot(sep_buf[2, row_block], pivot1[1, 0].reshape(rows, BLOCK)) for row_block in range(X)]
    even, odd = [state2[pair] - by_half(updates[pair], updates[pair + 2]) for pair in range(2)]
    moved_even, moved_odd = turned(even, -1), turned(odd, 1)
    pack3[0] = by_group([even, moved_odd, even, moved_odd])
    pack3[1] = by_group([moved_even, odd, moved_even, odd])
    give3[...] = pack3[1 - bit(3)].astype(BF16)
    y_copies.append(remote(give3, take3, y_sem, (X + 1,), {"layer": partner(3)}))
    y_copies[-1].start()
    y_copies[-1].wait_recv()
    value = pack3[bit(3)] + take3[...].astype(F32)
    state3[...] = value
    picked = by_group([weight(3, g) * value for g in range(X)])
    picked = picked + turned(picked, 1)
    picked = picked + turned(picked, 2)
    cand1[2, 0] = picked.astype(BF16).reshape(Z, rows // Z, BLOCK)
    spread(3, cand1.at[2], parts1.at[2], pivot1.at[2])
    for copy in sep_copies[3]:
        copy.wait_recv()
    updates = [dot(sep_buf[3, row_block], pivot1[2, 0].reshape(rows, BLOCK)) for row_block in range(X)]
    value = state3[...] - by_group(updates)

    quarter = rows // X
    for row_block in range(X):
        slices[row_block] = by_group(
            [turned(value[k * quarter : (k + 1) * quarter], k - row_block) for k in range(X)]
        )
    final_copies = []
    for d in range(1, X):
        final_copies.append(remote(slices.at[along_x(d)], final.at[x], final_sem, (d - 1,), to_x(d)))
        final_copies[-1].start()
    final[x] = slices[x]
    for copy in final_copies:
        copy.wait_recv()
    for k in range(X):
        out_ref[k * quarter : (k + 1) * quarter, :] = by_group([turned(final[q], q - k) for q in range(X)])

    started = u_copies + mask_copies + l_copies + list(ring.values()) + core_copies + y_copies + final_copies
    for copy in started + [copy for level in sep_copies for copy in level]:
        copy.wait_send()


def local(l_panels, u_panels, panel_fill, copy_fill, sep_panels, sep_owner):
    _, panels, rows, width = l_panels.shape
    depth, columns = u_panels.shape[2:]
    quarter = columns // X
    remote_sems = [
        (X - 1,), (X - 1,), (6,), (Z,), (X,), (LEVELS, X - 1), None, (X + 2,), (LEVELS, Z), (LEVELS, Z), (X - 1,),
    ]
    smem = pl.BlockSpec(memory_space=pltpu.SMEM)
    vmem = pl.BlockSpec(memory_space=pltpu.VMEM)
    return pl.pallas_call(
        kernel,
        out_shape=jax.ShapeDtypeStruct((rows, BLOCK), F32),
        in_specs=[smem, smem, smem, vmem, vmem, pl.BlockSpec(memory_space=pl.ANY)],
        out_specs=vmem,
        scratch_shapes=[
            pltpu.VMEM((X, panels, depth, quarter), BF16),
            pltpu.VMEM((panels, X, Z, depth, quarter), BF16),
            pltpu.VMEM((X, rows, panels * width), BF16),
            pltpu.VMEM((X, 8, quarter), F32),
            pltpu.VMEM((2, X, rows, 2 * BLOCK), F32),
            pltpu.VMEM((X, rows, 2 * BLOCK), F32),
            pltpu.VMEM((2, X, rows, BLOCK), F32),
            pltpu.VMEM((LEVELS, X, rows, sep_panels.shape[2]), BF16),
            pltpu.VMEM((X, rows, BLOCK), BF16),
            pltpu.VMEM((X, rows, BLOCK), BF16),
            pltpu.VMEM((X, rows, BLOCK), F32),
            pltpu.VMEM((2, 2, rows, BLOCK), F32),
            pltpu.VMEM((2, rows, BLOCK), BF16),
            pltpu.VMEM((2, rows, BLOCK), BF16),
            pltpu.VMEM((2, rows, BLOCK), F32),
            pltpu.VMEM((2, rows, BLOCK), F32),
            pltpu.VMEM((rows, BLOCK), BF16),
            pltpu.VMEM((rows, BLOCK), BF16),
            pltpu.VMEM((rows, BLOCK), F32),
            pltpu.VMEM((2, Z, rows // Z, BLOCK), BF16),
            pltpu.VMEM((Z, 2, rows // Z, BLOCK), BF16),
            pltpu.VMEM((2, Z, rows // Z, BLOCK), BF16),
            pltpu.VMEM((3, 1, Z, rows // Z, BLOCK), BF16),
            pltpu.VMEM((3, Z, 1, rows // Z, BLOCK), BF16),
            pltpu.VMEM((3, 1, Z, rows // Z, BLOCK), BF16),
            pltpu.VMEM((X, rows // X, BLOCK), F32),
            pltpu.VMEM((X, rows // X, BLOCK), F32),
            *[pltpu.SemaphoreType.DMA((LEVELS,) if s is None else (2, *s)) for s in remote_sems],
        ],
        compiler_params=pltpu.CompilerParams(
            collective_id=0, has_side_effects=True, vmem_limit_bytes=40 * 2**20
        ),
        cost_estimate=pl.CostEstimate(flops=2**31, bytes_accessed=2**22, transcendentals=0),
    )(sep_owner, panel_fill, copy_fill, l_panels, u_panels, sep_panels)


def solution(mesh):
    return jax.shard_map(
        local,
        mesh=mesh,
        in_specs=(
            P("layer", None, "grid", None),
            P("layer", None, "grid", None),
            P("layer", None, "grid", None),
            P("layer", "grid", None),
            P(None, "grid", None),
            P(),
        ),
        out_specs=P("grid", "layer"),
        check_vma=False,
    )
```

time: 1020 us -> 116 us (0.11)
  waiting for transfers between devices: 944 us -> 0 us
  Pallas kernels: 0 us -> 109 us
  other arithmetic: 21 us -> 0 us
  matrix products: 17.7 us -> 0 us
  between operations: 15.7 us -> 0.02 us
  starting transfers between devices: 14.7 us -> 0 us
    psum x4 -> x0, waiting for transfers between devices: 640 us -> none  [spread(): return lax.psum(jnp.where(mine, x, jnp.zeros_like(x)), axis)]
    ppermute x4 -> x0, waiting for transfers between devices: 211 us -> none  [from_partner(): lax.ppermute(x, axis, [(i, i ^ 1 << apart) for i in range(lax.axis_size(a...]
    pallas_call x0 -> x1, Pallas kernels: none -> 109 us  [local(): pl.pallas_call(kernel, out_shape=jax.ShapeDtypeStruct((rows, BLOCK), F32)...]
    all_gather x1 -> x0, waiting for transfers between devices: 92.7 us -> none  [local(): piece = lax.all_gather(u_panels, 'grid', axis=2, tiled=True)]
    dot_general x6 -> x0, matrix products: 17.7 us -> none  [the longest x4 12.7 us: local(): jnp.dot(factor, pivot_rows, preferred_element_type=jnp.float32)]
    select_n x4 -> x0, other arithmetic: 17.7 us -> none  [spread(): return lax.psum(jnp.where(mine, x, jnp.zeros_like(x)), axis)]
    ppermute x4 -> x0, starting transfers between devices: 14.5 us -> none  [from_partner(): lax.ppermute(x, axis, [(i, i ^ 1 << apart) for i in range(lax.axis_size(a...]
  transfers between devices with their start and end apart: 9 -> 0, of which waited for: 9 -> 0; matrix products, arithmetic and copies ran while one was open for 0% -> 0% of each run, Pallas kernels for 0% -> 0%
where the time goes in v2:
time: 116 us; the launch traced here: 115 us
  Pallas kernels  109 us (94%)
  local copies, waits for them, and re-layouts  6.16 us (5%)
    pallas_call x1, Pallas kernels, local(): pl.pallas_call(kernel, out_shape=jax.ShapeDtypeStruct((rows, BLOCK), F32)...  109 us
    unnamed x13, local copies, waits for them, and re-layouts  6.16 us

profile of v2, /device:TPU:56, one launch (start us, length us, event | category | flops | bytes accessed | tf_op | source)
XLA Modules:
  0.0 114.8 jit_solution(9761806631509381398)
XLA Ops:
  0.0 0.0 copy-start
  0.0 1.5 %copy-done = bf16[15,256,256]{2,1,0:T(8,128)(2,1)S(1)} copy-done((bf16[15,256,256]{2,1,0:T(8,128)(2,1)S(1)}, bf16[15,256,256]{2,1,0:T(8,128)(2,1)}, u32[]{:S(2)}) %copy-start) | copy-done | bytes 1966104
  1.5 0.0 copy-start.1
  1.5 1.0 copy-done.1
  2.6 0.0 copy-start.2
  2.6 0.9 copy-done.2
  3.5 0.0 copy-start.3
  3.5 0.7 copy-done.3
  4.2 0.0 copy-start.4
  4.2 0.7 copy-done.4
  4.9 0.0 copy-start.5
  4.9 0.7 copy-done.5
  5.5 108.6 %shard_map.64 = f32[256,128]{1,0:T(8,128)S(1)} custom-call(s32[15]{0:T(128)S(1)} %copy-done.5, s32[1,2,2,4]{3,2,1,0:T(2,128)S(1)} %copy-done.3, s32[1,2,16]{2,1,0:T(2,128)S(1)} %copy-done.4, bf16[1,2,256,512]{3,2,1,0:T(8,128)(2,1)S(1)} %copy-done.1, bf16[1,2,16,2048]{3,2,1,0:T(8,128)(2,1)S(1)} %copy-done.2, bf16[15,256,256]{2,1,0:T(8,128)(2,1)S(1)} %copy-done), custom_call_target="tpu_custom_call" | custom-call | flops 2147483648 | bytes 4194304 | tf_op jit(solution)/shard_map/pallas_call | solution.py:341
  114.2 0.7 copy.8
Async XLA Ops:
  0.0 1.5 %copy-start = (bf16[15,256,256]{2,1,0:T(8,128)(2,1)S(1)}, bf16[15,256,256]{2,1,0:T(8,128)(2,1)}, u32[]{:S(2)}) copy-start(bf16[15,256,256]{2,1,0:T(8,128)(2,1)} %sep_ref.1) | copy-start | bytes 5898244
  1.5 1.0 copy-start.1
  2.6 0.9 copy-start.2
  3.5 0.7 copy-start.3
  4.2 0.7 copy-start.4
  4.9 0.7 copy-start.5

commit v3 on v2

v3 whole, which is shorter than its diff:
```python
import jax
import jax.numpy as jnp
from jax import lax
from jax.experimental import pallas as pl
from jax.experimental.pallas import tpu as pltpu
from jax.sharding import PartitionSpec as P

BLOCK = 128
X = 4
Z = 8
GROUP = BLOCK // X
LEVELS = 4
F32 = jnp.float32
BF16 = jnp.bfloat16


def turned(v, groups):
    shift = groups % X * GROUP
    return pltpu.roll(v, shift, 1) if shift else v


def by_group(pieces):
    group = lax.broadcasted_iota(jnp.int32, pieces[0].shape, 1) // GROUP
    out = pieces[0]
    for g in range(1, X):
        out = jnp.where(group == g, pieces[g], out)
    return out


def by_half(low, high):
    lane = lax.broadcasted_iota(jnp.int32, low.shape, 1)
    return jnp.where(lane < BLOCK // 2, low, high)


def column_block(tile, group):
    return (tile >> 1) + 2 * (tile & 1) + 4 * (group >> 1) + 8 * (group & 1)


def dot(a, b):
    return jnp.dot(a, b, preferred_element_type=F32)


def kernel(
    owner_any, panel_fill_any, copy_fill_any, l_any, u_any, sep_ref, out_ref,
    owner_ref, panel_fill_ref, copy_fill_ref, l_ref, u_ref,
    u_row, u_buf, l_buf, mask, acc, other, half, sep_buf,
    give1, take1, state1, pack2, give2, take2, state2, pack3, give3, take3, state3,
    cand0, parts0, chunk0, pivot0, cand1, parts1, chunk1, pivot1, cand2, parts2, chunk2, pivot2, cand3, parts3,
    slices, final,
    u_sem, mask_sem, l_sem, ring_sem, core_sem, sep_sem, pass_sem, own_sem, y_sem, part_sem, pivot_sem, final_sem,
):
    layer = lax.axis_index("layer")
    grid = lax.axis_index("grid")
    x = grid // Z
    z = grid % Z
    rows = l_ref.shape[2]
    width = l_ref.shape[3]
    panels = l_ref.shape[1]
    depth = u_ref.shape[2]

    def along_x(d):
        return (x + d) % X

    def along_z(d):
        return (z + d) % Z

    def bit(level):
        return layer // 2**level % 2

    def partner(level):
        return layer + 2**level * (1 - 2 * bit(level))

    def remote(src, dst, sems, index, device):
        return pltpu.make_async_remote_copy(
            src_ref=src,
            dst_ref=dst,
            send_sem=sems.at[(0, *index)],
            recv_sem=sems.at[(1, *index)],
            device_id=device,
            device_id_type=pl.DeviceIdType.MESH,
        )

    def to_x(d):
        return {"grid": along_x(d) * Z + z}

    def to_z(d):
        return {"grid": x * Z + along_z(d)}

    def across(level, d):
        return {"layer": partner(level), "grid": x * Z + along_z(d)}

    def node(level, sibling):
        group = layer // 2 ** (level + 1)
        if sibling:
            group = group + 1 - 2 * (group % 2)
        return 2**LEVELS - (2**LEVELS >> level) + group

    barrier = pltpu.get_barrier_semaphore()
    peers = [to_x(d) for d in range(1, X)] + [to_z(d) for d in range(1, Z)]
    peers += [across(0, 0)] + [across(level, d) for level in range(1, LEVELS) for d in range(Z)]
    for peer in peers:
        pl.semaphore_signal(barrier, inc=1, device_id=peer, device_id_type=pl.DeviceIdType.MESH)

    pairs = ((u_any, u_ref), (panel_fill_any, panel_fill_ref), (l_any, l_ref), (copy_fill_any, copy_fill_ref), (owner_any, owner_ref))
    loads = [pltpu.make_async_copy(src, dst, own_sem.at[i]) for i, (src, dst) in enumerate(pairs)]
    for load in loads:
        load.start()
    load_u, load_panel_fill, load_l, load_copy_fill, load_owner = loads
    items = [(level, sibling) for level in range(LEVELS) for sibling in range(2)][:-1]
    own_sep = []
    for i, (level, sibling) in enumerate(items):
        own_sep.append(
            pltpu.make_async_copy(sep_ref.at[node(level, sibling)], sep_buf.at[i, x], own_sem.at[len(loads) + i])
        )
        own_sep[i].start()

    load_u.wait()
    turns = {}
    for tile in range(X):
        for group in range(X):
            block = column_block(tile, group)
            piece = u_ref[0, :, :, block * BLOCK : (block + 1) * BLOCK].astype(F32).reshape(panels * depth, BLOCK)
            turns[tile, group] = [turned(piece, n) for n in range(X)]
        for quarter in range(X):
            mixed = by_group([turns[tile, group][(group - quarter) % X] for group in range(X)])
            u_row[quarter, :, :, tile * BLOCK : (tile + 1) * BLOCK] = mixed.astype(BF16).reshape(panels, depth, BLOCK)
    u_buf[:, x, z] = u_row[x]

    load_panel_fill.wait()
    load_l.wait()
    for r in range(rows // BLOCK):
        for k in range(panels):
            for c in range(width // BLOCK):
                fill = panel_fill_ref[0, k, r, c].astype(F32)
                piece = l_ref[0, k, r * BLOCK : (r + 1) * BLOCK, c * BLOCK : (c + 1) * BLOCK].astype(F32) * fill
                l_buf[x, r * BLOCK : (r + 1) * BLOCK, k * width + c * BLOCK : k * width + (c + 1) * BLOCK] = (
                    piece.astype(BF16)
                )

    load_copy_fill.wait()
    load_owner.wait()
    shape = (8, BLOCK)
    sublane = lax.broadcasted_iota(jnp.int32, shape, 0)
    for tile in range(X):
        picked = []
        for group in range(X):
            value = jnp.zeros(shape, F32)
            for r in range(rows // BLOCK):
                fill = copy_fill_ref[0, r, column_block(tile, group)].astype(F32)
                value = jnp.where(sublane == r, -fill, value)
            picked.append(value)
        mask[x, :, tile * BLOCK : (tile + 1) * BLOCK] = by_group(picked)

    pl.semaphore_wait(barrier, len(peers))

    u_copies = []
    for d in range(1, X):
        u_copies.append(remote(u_row.at[along_x(d)], u_buf.at[:, x, z], u_sem, (d - 1,), to_x(d)))
        u_copies[-1].start()

    def ring_copy(step, index, way):
        block = along_z(-way * (step - 1))
        source = along_x((0, -1, 1, 2)[index])
        if step < Z // 2:
            where = u_buf.at[:, source, block]
        else:
            where = u_buf.at[0 if way > 0 else 1, source, block]
        return remote(where, where, ring_sem, (Z * index + 2 * (step - 1) + (way < 0),), to_z(way))

    ring = {}

    def ring_step(step, index):
        if step == 1 and index:
            u_copies[(None, 0, 2, 1)[index]].wait_recv()
        for way in (1, -1):
            if step > 1:
                ring[step - 1, index, way].wait_recv()
            if step <= Z // 2:
                ring[step, index, way] = ring_copy(step, index, way)
                ring[step, index, way].start()

    ring_step(1, 0)

    def l_copy(index, source, part, d):
        where = l_buf.at[along_x(source), pl.ds(part * BLOCK, BLOCK)]
        return remote(where, where, l_sem, (index,), to_x(d))

    l_copies = [l_copy(0, 0, 0, 1), l_copy(1, 0, 1, -1), l_copy(2, 0, 1, 1), l_copy(3, 0, 0, -1)]
    for copy in l_copies:
        copy.start()
    mask_copies = []
    for d in range(1, X):
        mask_copies.append(remote(mask.at[x], mask.at[x], mask_sem, (d - 1,), to_x(d)))
        mask_copies[-1].start()

    for index in range(1, X):
        ring_step(1, index)
    for step in range(2, Z // 2 + 2):
        for index in range(X):
            ring_step(step, index)
        if step == 2:
            for index, (source, part, way) in enumerate(((-1, 0, 1), (1, 1, -1))):
                l_copies[index].wait_recv()
                l_copies.append(l_copy(4 + index, source, part, way))
                l_copies[-1].start()

    way = 1 - 2 * bit(0)
    beside, opposite = along_x(-way), along_x(2)

    sep_copies = [[] for _ in items]

    def sep_copy(i, where, sems, index, device):
        sep_copies[i].append(remote(where, where, sems, (i, index), device))
        sep_copies[i][-1].start()

    def sep_start(i):
        own_sep[i].wait()
        sep_copy(i, sep_buf.at[i, x], sep_sem, 0, to_x(way))

    def sep_forward(i):
        sep_copies[i][0].wait_recv()
        sep_copy(i, sep_buf.at[i, beside, pl.ds(bit(0) * BLOCK, BLOCK)], sep_sem, 1, to_x(way))
        sep_copy(i, sep_buf.at[i, beside], pass_sem, 0, across(0, 0))

    def sep_finish(i):
        sep_copies[i][1].wait_recv()
        sep_copy(i, sep_buf.at[i, opposite, pl.ds(bit(0) * BLOCK, BLOCK)], pass_sem, 1, across(0, 0))

    def sep_wait(i):
        sep_copies[i][2].wait_recv()
        sep_copies[i][3].wait_recv()

    for copy in mask_copies:
        copy.wait_recv()

    def weight(level, row_block):
        return jnp.where(owner_ref[node(level, 0)] == row_block * Z + z, 1.0, 0.0).astype(F32)

    core_copies = []
    y_copies = []
    order = [along_x(d) for d in (0, -1, 1, 2)]
    waits = [[], [2], [3], [4, 5]]
    giving = 1 - bit(1)
    total0 = [jnp.zeros((rows, BLOCK), F32) for _ in range(2)]
    for index in range(X + 1):
        if index < X:
            row_block = order[index]
            for which in waits[index]:
                l_copies[which].wait_recv()
            if index == X - 1:
                sep_start(0)
                sep_start(1)
            u_all = u_buf[...].reshape(panels * width, X * BLOCK)
            for r in range(rows // BLOCK):
                part = dot(l_buf[row_block, r * BLOCK : (r + 1) * BLOCK], u_all) * mask[row_block, r : r + 1]
                for h in range(2):
                    acc[h, row_block, r * BLOCK : (r + 1) * BLOCK] = part[:, h * 2 * BLOCK : (h + 1) * 2 * BLOCK]
            core_copies.append(
                remote(acc.at[1 - bit(0), row_block], other.at[row_block], core_sem, (index,), across(0, 0))
            )
            core_copies[-1].start()
        if index:
            row_block = order[index - 1]
            core_copies[index - 1].wait_recv()
            value = acc[bit(0), row_block] + other[row_block]
            for h in range(2):
                half[h, row_block] = value[:, h * BLOCK : (h + 1) * BLOCK]
                total0[h] = total0[h] + weight(0, row_block) * value[:, h * BLOCK : (h + 1) * BLOCK]
            give1[row_block] = half[giving, row_block].astype(BF16)
            y_copies.append(remote(give1.at[row_block], take1.at[row_block], y_sem, (index - 1,), across(1, 0)))
            y_copies[-1].start()

    late = []

    def each(low, act):
        def body(d, carry):
            act(d)
            return carry

        lax.fori_loop(low, Z, body, 0)

    def part_copies(level, cand, parts):
        return lambda d: remote(cand.at[along_z(d)], parts.at[d], part_sem, (level, d), to_z(d))

    def add_parts(own, parts, copies):
        def add(d, total):
            copies(d).wait_recv()
            return total + parts[d].astype(F32)

        total = lax.fori_loop(1, Z, add, own.astype(F32))
        late.append((1, copies))
        return total

    def pivot_start(level, mine, theirs, pivot):
        def here(d):
            return remote(mine, pivot.at[0, z], pivot_sem, (level, d), to_z(d))

        def there(d):
            return remote(theirs, pivot.at[1, z], pivot_sem, (level, Z + d), across(level + 1, d))

        each(1, lambda d: here(d).start())
        each(0, lambda d: there(d).start())
        pivot[0, z] = mine[...]
        return here, there

    def pivot_wait(copies):
        here, there = copies
        each(1, lambda d: here(d).wait_recv())
        each(0, lambda d: there(d).wait_recv())
        late.extend([(1, here), (0, there)])

    def update(level, row_block, pivots):
        return sum(dot(sep_buf[2 * level + i, row_block], pivot) for i, pivot in enumerate(pivots))

    for h in range(2):
        cand0[:, h] = total0[h].astype(BF16).reshape(Z, rows // Z, BLOCK)
    copies = part_copies(0, cand0, parts0)
    each(1, lambda d: copies(d).start())
    for i in (0, 1):
        sep_forward(i)
    for i in range(2, len(items)):
        sep_start(i)
    chunk0[...] = add_parts(cand0[z], parts0, copies).astype(BF16)
    copies = pivot_start(0, chunk0.at[bit(1)], chunk0.at[giving], pivot0)
    for i in (0, 1):
        sep_finish(i)
    for i in (0, 1):
        sep_wait(i)
    pivot_wait(copies)

    picked = jnp.zeros((rows, BLOCK), F32)
    pivots = [pivot0[i].reshape(rows, BLOCK) for i in range(2)]
    for copy in y_copies:
        copy.wait_recv()
    for row_block in range(X):
        value = half[bit(1), row_block] - update(0, row_block, pivots)
        value = value + take1[row_block].astype(F32)
        state1[row_block] = value
        picked = picked + weight(1, row_block) * value
    cand1[...] = picked.astype(BF16).reshape(Z, rows // Z, BLOCK)
    copies = part_copies(1, cand1, parts1)
    each(1, lambda d: copies(d).start())

    def pack_two(blocks):
        for pair in range(2):
            low, high = blocks[pair], blocks[pair + 2]
            pack2[0, pair] = by_half(low, turned(high, 2))
            pack2[1, pair] = by_half(turned(low, 2), high)

    pack_two([state1[row_block] for row_block in range(X)])
    give2[...] = pack2[1 - bit(2)].astype(BF16)
    y_copies.append(remote(give2, take2, y_sem, (X,), across(2, 0)))
    y_copies[-1].start()
    for i in (2, 3):
        sep_forward(i)
    chunk1[...] = add_parts(cand1[z], parts1, copies).astype(BF16)
    copies = pivot_start(1, chunk1, chunk1, pivot1)
    for i in (2, 3):
        sep_finish(i)
    for i in (2, 3):
        sep_wait(i)
    pivot_wait(copies)

    pivots = [pivot1[i].reshape(rows, BLOCK) for i in range(2)]
    pack_two([state1[row_block] - update(1, row_block, pivots) for row_block in range(X)])
    y_copies[-1].wait_recv()
    value = pack2[bit(2)] + take2[...].astype(F32)
    state2[...] = value
    picked = by_half(*[weight(2, 2 * h) * value[0] + weight(2, 2 * h + 1) * value[1] for h in range(2)])
    picked = picked + turned(picked, 2)
    picked = by_half(picked[: rows // 2], picked[rows // 2 :])
    cand2[...] = picked.astype(BF16).reshape(Z, rows // Z // 2, BLOCK)
    copies = part_copies(2, cand2, parts2)
    each(1, lambda d: copies(d).start())

    def pack_four(even, odd):
        moved_even, moved_odd = turned(even, -1), turned(odd, 1)
        pack3[0] = by_group([even, moved_odd, even, moved_odd])
        pack3[1] = by_group([moved_even, odd, moved_even, odd])

    pack_four(state2[0], state2[1])
    give3[...] = pack3[1 - bit(3)].astype(BF16)
    y_copies.append(remote(give3, take3, y_sem, (X + 1,), across(3, 0)))
    y_copies[-1].start()
    for i in (4, 5, 6):
        sep_forward(i)
    chunk2[...] = add_parts(cand2[z], parts2, copies).astype(BF16)
    copies = pivot_start(2, chunk2, chunk2, pivot2)
    for i in (4, 5, 6):
        sep_finish(i)
    for i in (4, 5, 6):
        sep_wait(i)
    pivot_wait(copies)

    pivots = []
    for i in range(2):
        packed = pivot2[i].astype(F32).reshape(rows // 2, BLOCK)
        moved = turned(packed, 2)
        pivots.append(jnp.concatenate([by_half(packed, moved), by_half(moved, packed)], axis=0).astype(BF16))
    updates = [update(2, row_block, pivots) for row_block in range(X)]
    pack_four(*[state2[pair] - by_half(updates[pair], updates[pair + 2]) for pair in range(2)])
    y_copies[-1].wait_recv()
    value = pack3[bit(3)] + take3[...].astype(F32)
    state3[...] = value
    picked = by_group([weight(3, g) * value for g in range(X)])
    picked = picked + turned(picked, 1)
    picked = picked + turned(picked, 2)
    quarter = rows // X
    cand3[...] = by_group([picked[k * quarter : (k + 1) * quarter] for k in range(X)]).astype(BF16)

    def whole_copies(d):
        return remote(cand3, parts3.at[d], part_sem, (3, d), to_z(d))

    each(1, lambda d: whole_copies(d).start())
    packed = add_parts(cand3[...], parts3, whole_copies)
    pivot = []
    for k in range(X):
        nothing = jnp.zeros_like(packed)
        one = by_group([packed if g == k else nothing for g in range(X)])
        one = one + turned(one, 1)
        pivot.append(one + turned(one, 2))
    pivot = jnp.concatenate(pivot, axis=0).astype(BF16)
    value = state3[...] - by_group([update(3, row_block, [pivot]) for row_block in range(X)])

    for row_block in range(X):
        slices[row_block] = by_group(
            [turned(value[k * quarter : (k + 1) * quarter], k - row_block) for k in range(X)]
        )
    final_copies = []
    for d in range(1, X):
        final_copies.append(remote(slices.at[along_x(d)], final.at[x], final_sem, (d - 1,), to_x(d)))
        final_copies[-1].start()
    final[x] = slices[x]
    for copy in final_copies:
        copy.wait_recv()
    for k in range(X):
        out_ref[k * quarter : (k + 1) * quarter, :] = by_group([turned(final[q], q - k) for q in range(X)])

    started = u_copies + mask_copies + l_copies + list(ring.values()) + core_copies + y_copies + final_copies
    for copy in started + [copy for item in sep_copies for copy in item]:
        copy.wait_send()
    for low, copies in late:
        each(low, lambda d, copies=copies: copies(d).wait_send())


def local(l_panels, u_panels, panel_fill, copy_fill, sep_panels, sep_owner):
    _, panels, rows, width = l_panels.shape
    depth, columns = u_panels.shape[2:]
    quarter = columns // X
    items = 2 * LEVELS - 1
    remote_sems = [
        (X - 1,), (X - 1,), (6,), (X * Z,), (X,), (items, 2), (items, 2), None, (X + 2,), (LEVELS, Z),
        (LEVELS - 1, 2 * Z), (X - 1,),
    ]
    chunk = rows // Z
    kept = pl.BlockSpec(memory_space=pl.ANY)
    return pl.pallas_call(
        kernel,
        out_shape=jax.ShapeDtypeStruct((rows, BLOCK), F32),
        in_specs=[kept] * 6,
        out_specs=pl.BlockSpec(memory_space=pltpu.VMEM),
        scratch_shapes=[
            pltpu.SMEM(sep_owner.shape, jnp.int32),
            pltpu.SMEM(panel_fill.shape, jnp.int32),
            pltpu.SMEM(copy_fill.shape, jnp.int32),
            pltpu.VMEM(l_panels.shape, BF16),
            pltpu.VMEM(u_panels.shape, BF16),
            pltpu.VMEM((X, panels, depth, quarter), BF16),
            pltpu.VMEM((panels, X, Z, depth, quarter), BF16),
            pltpu.VMEM((X, rows, panels * width), BF16),
            pltpu.VMEM((X, 8, quarter), F32),
            pltpu.VMEM((2, X, rows, 2 * BLOCK), F32),
            pltpu.VMEM((X, rows, 2 * BLOCK), F32),
            pltpu.VMEM((2, X, rows, BLOCK), F32),
            pltpu.VMEM((items, X, rows, sep_panels.shape[2]), BF16),
            pltpu.VMEM((X, rows, BLOCK), BF16),
            pltpu.VMEM((X, rows, BLOCK), BF16),
            pltpu.VMEM((X, rows, BLOCK), F32),
            pltpu.VMEM((2, 2, rows, BLOCK), F32),
            pltpu.VMEM((2, rows, BLOCK), BF16),
            pltpu.VMEM((2, rows, BLOCK), BF16),
            pltpu.VMEM((2, rows, BLOCK), F32),
            pltpu.VMEM((2, rows, BLOCK), F32),
            pltpu.VMEM((rows, BLOCK), BF16),
            pltpu.VMEM((rows, BLOCK), BF16),
            pltpu.VMEM((rows, BLOCK), F32),
            pltpu.VMEM((Z, 2, chunk, BLOCK), BF16),
            pltpu.VMEM((Z, 2, chunk, BLOCK), BF16),
            pltpu.VMEM((2, chunk, BLOCK), BF16),
            pltpu.VMEM((2, Z, chunk, BLOCK), BF16),
            pltpu.VMEM((Z, chunk, BLOCK), BF16),
            pltpu.VMEM((Z, chunk, BLOCK), BF16),
            pltpu.VMEM((chunk, BLOCK), BF16),
            pltpu.VMEM((2, Z, chunk, BLOCK), BF16),
            pltpu.VMEM((Z, chunk // 2, BLOCK), BF16),
            pltpu.VMEM((Z, chunk // 2, BLOCK), BF16),
            pltpu.VMEM((chunk // 2, BLOCK), BF16),
            pltpu.VMEM((2, Z, chunk // 2, BLOCK), BF16),
            pltpu.VMEM((rows // X, BLOCK), BF16),
            pltpu.VMEM((Z, rows // X, BLOCK), BF16),
            pltpu.VMEM((X, rows // X, BLOCK), F32),
            pltpu.VMEM((X, rows // X, BLOCK), F32),
            *[pltpu.SemaphoreType.DMA((items + 5,) if s is None else (2, *s)) for s in remote_sems],
        ],
        compiler_params=pltpu.CompilerParams(
            collective_id=0, has_side_effects=True, vmem_limit_bytes=60 * 2**20
        ),
        cost_estimate=pl.CostEstimate(flops=2**31, bytes_accessed=2**22, transcendentals=0),
    )(sep_owner, panel_fill, copy_fill, l_panels, u_panels, sep_panels)


def solution(mesh):
    return jax.shard_map(
        local,
        mesh=mesh,
        in_specs=(
            P("layer", None, "grid", None),
            P("layer", None, "grid", None),
            P("layer", None, "grid", None),
            P("layer", "grid", None),
            P(None, "grid", None),
            P(),
        ),
        out_specs=P("grid", "layer"),
        check_vma=False,
    )
```

time: 116 us -> 92.8 us (0.80)
  Pallas kernels: 109 us -> 91.1 us
  local copies, waits for them, and re-layouts: 6.16 us -> 1.57 us
    pallas_call x1, Pallas kernels: 109 us -> 91.1 us  [local(): pl.pallas_call(kernel, out_shape=jax.ShapeDtypeStruct((rows, BLOCK), F32)...]
    unnamed x13 -> x1, local copies, waits for them, and re-layouts: 6.16 us -> 1.57 us
where the time goes in v3:
time: 92.8 us; the launch traced here: 92.7 us
  Pallas kernels  91.1 us (98%)
  local copies, waits for them, and re-layouts  1.57 us (2%)
    pallas_call x1, Pallas kernels, local(): pl.pallas_call(kernel, out_shape=jax.ShapeDtypeStruct((rows, BLOCK), F32)...  91.1 us

profile of v3, /device:TPU:56, one launch (start us, length us, event | category | flops | bytes accessed | tf_op | source)
XLA Modules:
  0.0 92.7 jit_solution(10939926619944136820)
XLA Ops:
  0.0 91.1 %shard_map.64 = f32[256,128]{1,0:T(8,128)} custom-call(s32[15]{0:T(128)} %owner_any.1, s32[1,2,2,4]{3,2,1,0:T(2,128)} %panel_fill_any.1, s32[1,2,16]{2,1,0:T(2,128)} %copy_fill_any.1, bf16[1,2,256,512]{3,2,1,0:T(8,128)(2,1)} %l_any.1, bf16[1,2,16,2048]{3,2,1,0:T(8,128)(2,1)} %u_any.1, bf16[15,256,256]{2,1,0:T(8,128)(2,1)} %sep_ref.1), custom_call_target="tpu_custom_call" | custom-call | flops 2147483648 | bytes 4194304 | tf_op jit(solution)/shard_map/pallas_call | solution.py:457
  91.1 1.6 %copy.8 = f32[256,128]{1,0:T(8,128)} copy(f32[256,128]{1,0:T(8,128)} %shard_map.64) | data formatting | bytes 262144

commit v4 on v3

--- a/solution.py
+++ b/solution.py
@@ -46,8 +46,9 @@
     u_row, u_buf, l_buf, mask, acc, other, half, sep_buf,
     give1, take1, state1, pack2, give2, take2, state2, pack3, give3, take3, state3,
     cand0, parts0, chunk0, pivot0, cand1, parts1, chunk1, pivot1, cand2, parts2, chunk2, pivot2, cand3, parts3,
-    slices, final,
+    slices, final, corner, corner_parts, corner_chunk, pack_chunk,
     u_sem, mask_sem, l_sem, ring_sem, core_sem, sep_sem, pass_sem, own_sem, y_sem, part_sem, pivot_sem, final_sem,
+    corner_sem, corner_pass_sem, ready_sem,
 ):
     layer = lax.axis_index("layer")
     grid = lax.axis_index("grid")
@@ -97,7 +98,7 @@
 
     barrier = pltpu.get_barrier_semaphore()
     peers = [to_x(d) for d in range(1, X)] + [to_z(d) for d in range(1, Z)]
-    peers += [across(0, 0)] + [across(level, d) for level in range(1, LEVELS) for d in range(Z)]
+    peers += [across(level, 0) for level in range(LEVELS)]
     for peer in peers:
         pl.semaphore_signal(barrier, inc=1, device_id=peer, device_id_type=pl.DeviceIdType.MESH)
 
@@ -152,6 +153,10 @@
         mask[x, :, tile * BLOCK : (tile + 1) * BLOCK] = by_group(picked)
 
     pl.semaphore_wait(barrier, len(peers))
+    for level in range(1, LEVELS):
+        pl.semaphore_signal(
+            ready_sem.at[level], inc=1, device_id=across(level, 0), device_id_type=pl.DeviceIdType.MESH
+        )
 
     u_copies = []
     for d in range(1, X):
@@ -318,12 +323,18 @@
     each(1, lambda d: copies(d).start())
     for i in (0, 1):
         sep_forward(i)
-    for i in range(2, len(items)):
+    for i in (2, 3):
         sep_start(i)
     chunk0[...] = add_parts(cand0[z], parts0, copies).astype(BF16)
+    for level in range(1, LEVELS):
+        pl.semaphore_wait(ready_sem.at[level], 1)
     copies = pivot_start(0, chunk0.at[bit(1)], chunk0.at[giving], pivot0)
     for i in (0, 1):
         sep_finish(i)
+    for i in (2, 3):
+        sep_forward(i)
+    for i in (4, 5, 6):
+        sep_start(i)
     for i in (0, 1):
         sep_wait(i)
     pivot_wait(copies)
@@ -341,37 +352,59 @@
     copies = part_copies(1, cand1, parts1)
     each(1, lambda d: copies(d).start())
 
-    def pack_two(blocks):
-        for pair in range(2):
-            low, high = blocks[pair], blocks[pair + 2]
-            pack2[0, pair] = by_half(low, turned(high, 2))
-            pack2[1, pair] = by_half(turned(low, 2), high)
-
-    pack_two([state1[row_block] for row_block in range(X)])
+    def pack_two(blocks, store):
+        pairs = len(blocks) // 2
+        for pair in range(pairs):
+            low, high = blocks[pair], blocks[pair + pairs]
+            store[0, pair] = by_half(low, turned(high, 2))
+            store[1, pair] = by_half(turned(low, 2), high)
+
+    pack_two([state1[row_block] for row_block in range(X)], pack2)
     give2[...] = pack2[1 - bit(2)].astype(BF16)
     y_copies.append(remote(give2, take2, y_sem, (X,), across(2, 0)))
     y_copies[-1].start()
     for i in (2, 3):
-        sep_forward(i)
-    chunk1[...] = add_parts(cand1[z], parts1, copies).astype(BF16)
-    copies = pivot_start(1, chunk1, chunk1, pivot1)
-    for i in (2, 3):
         sep_finish(i)
     for i in (2, 3):
         sep_wait(i)
-    pivot_wait(copies)
-
-    pivots = [pivot1[i].reshape(rows, BLOCK) for i in range(2)]
-    pack_two([state1[row_block] - update(1, row_block, pivots) for row_block in range(X)])
+    block = sum(weight(2, row_block) * sep_buf[2 + bit(0), row_block].astype(F32) for row_block in range(X))
+    for h in range(2):
+        corner[:, h] = block[h * BLOCK : (h + 1) * BLOCK].astype(BF16).reshape(Z, rows // Z // 2, rows)
+
+    def corner_copies(d):
+        return remote(corner.at[along_z(d)], corner_parts.at[d], corner_sem, (0, d), to_z(d))
+
+    each(1, lambda d: corner_copies(d).start())
+
+    chunk1[...] = add_parts(cand1[z], parts1, copies).astype(BF16)
+    pivot_copies = pivot_start(1, chunk1, chunk1, pivot1)
+    for i in (4, 5, 6):
+        sep_forward(i)
+
     y_copies[-1].wait_recv()
     value = pack2[bit(2)] + take2[...].astype(F32)
     state2[...] = value
     picked = by_half(*[weight(2, 2 * h) * value[0] + weight(2, 2 * h + 1) * value[1] for h in range(2)])
     picked = picked + turned(picked, 2)
     picked = by_half(picked[: rows // 2], picked[rows // 2 :])
-    cand2[...] = picked.astype(BF16).reshape(Z, rows // Z // 2, BLOCK)
+    cand2[...] = picked.reshape(Z, rows // Z // 2, BLOCK)
     copies = part_copies(2, cand2, parts2)
     each(1, lambda d: copies(d).start())
+    mine = corner_chunk.at[bit(0)]
+    corner_chunk[bit(0)] = add_parts(corner[z], corner_parts, corner_copies).astype(BF16)
+    corner_pass = remote(mine, mine, corner_pass_sem, (0,), across(0, 0))
+    corner_pass.start()
+    corner_pass.wait_recv()
+    pivot_wait(pivot_copies)
+
+    pivots = [pivot1[i].reshape(rows, BLOCK) for i in range(2)]
+    taken = sum(dot(corner_chunk[i].reshape(rows // Z, rows), pivots[i]) for i in range(2))
+    pack_two([taken[: rows // Z // 2], taken[rows // Z // 2 :]], pack_chunk)
+    total = add_parts(cand2[z], parts2, copies)
+    chunk2[...] = (total - pack_chunk[bit(2), 0]).astype(BF16)
+    pivot_copies = pivot_start(2, chunk2, chunk2, pivot2)
+    pack_two([update(1, row_block, pivots) for row_block in range(X)], pack2)
+    state2[...] = state2[...] - pack2[bit(2)]
 
     def pack_four(even, odd):
         moved_even, moved_odd = turned(even, -1), turned(odd, 1)
@@ -383,14 +416,10 @@
     y_copies.append(remote(give3, take3, y_sem, (X + 1,), across(3, 0)))
     y_copies[-1].start()
     for i in (4, 5, 6):
-        sep_forward(i)
-    chunk2[...] = add_parts(cand2[z], parts2, copies).astype(BF16)
-    copies = pivot_start(2, chunk2, chunk2, pivot2)
-    for i in (4, 5, 6):
         sep_finish(i)
     for i in (4, 5, 6):
         sep_wait(i)
-    pivot_wait(copies)
+    pivot_wait(pivot_copies)
 
     pivots = []
     for i in range(2):
@@ -436,7 +465,7 @@
     for k in range(X):
         out_ref[k * quarter : (k + 1) * quarter, :] = by_group([turned(final[q], q - k) for q in range(X)])
 
-    started = u_copies + mask_copies + l_copies + list(ring.values()) + core_copies + y_copies + final_copies
+    started = [corner_pass] + u_copies + mask_copies + l_copies + list(ring.values()) + core_copies + y_copies + final_copies
     for copy in started + [copy for item in sep_copies for copy in item]:
         copy.wait_send()
     for low, copies in late:
@@ -450,7 +479,7 @@
     items = 2 * LEVELS - 1
     remote_sems = [
         (X - 1,), (X - 1,), (6,), (X * Z,), (X,), (items, 2), (items, 2), None, (X + 2,), (LEVELS, Z),
-        (LEVELS - 1, 2 * Z), (X - 1,),
+        (LEVELS - 1, 2 * Z), (X - 1,), (1, Z), (1,),
     ]
     chunk = rows // Z
     kept = pl.BlockSpec(memory_space=pl.ANY)
@@ -492,15 +521,20 @@
             pltpu.VMEM((Z, chunk, BLOCK), BF16),
             pltpu.VMEM((chunk, BLOCK), BF16),
             pltpu.VMEM((2, Z, chunk, BLOCK), BF16),
-            pltpu.VMEM((Z, chunk // 2, BLOCK), BF16),
-            pltpu.VMEM((Z, chunk // 2, BLOCK), BF16),
+            pltpu.VMEM((Z, chunk // 2, BLOCK), F32),
+            pltpu.VMEM((Z, chunk // 2, BLOCK), F32),
             pltpu.VMEM((chunk // 2, BLOCK), BF16),
             pltpu.VMEM((2, Z, chunk // 2, BLOCK), BF16),
             pltpu.VMEM((rows // X, BLOCK), BF16),
             pltpu.VMEM((Z, rows // X, BLOCK), BF16),
             pltpu.VMEM((X, rows // X, BLOCK), F32),
             pltpu.VMEM((X, rows // X, BLOCK), F32),
+            pltpu.VMEM((Z, 2, chunk // 2, rows), BF16),
+            pltpu.VMEM((Z, 2, chunk // 2, rows), BF16),
+            pltpu.VMEM((2, 2, chunk // 2, rows), BF16),
+            pltpu.VMEM((2, 1, chunk // 2, BLOCK), F32),
             *[pltpu.SemaphoreType.DMA((items + 5,) if s is None else (2, *s)) for s in remote_sems],
+            pltpu.SemaphoreType.REGULAR((LEVELS,)),
         ],
         compiler_params=pltpu.CompilerParams(
             collective_id=0, has_side_effects=True, vmem_limit_bytes=60 * 2**20

time: 92.8 us -> 87.6 us (0.944)
  Pallas kernels: 91.1 us -> 85.8 us
    pallas_call x1, Pallas kernels: 91.1 us -> 85.8 us  [local(): pl.pallas_call(kernel, out_shape=jax.ShapeDtypeStruct((rows, BLOCK), F32)...]
where the time goes in v4:
time: 87.6 us; the launch traced here: 87.3 us
  Pallas kernels  85.8 us (98%)
  local copies, waits for them, and re-layouts  1.57 us (2%)
    pallas_call x1, Pallas kernels, local(): pl.pallas_call(kernel, out_shape=jax.ShapeDtypeStruct((rows, BLOCK), F32)...  85.8 us

profile of v4, /device:TPU:56, one launch (start us, length us, event | category | flops | bytes accessed | tf_op | source)
XLA Modules:
  0.0 87.3 jit_solution(13106590933286628352)
XLA Ops:
  0.0 85.8 %shard_map.64 = f32[256,128]{1,0:T(8,128)} custom-call(s32[15]{0:T(128)} %owner_any.1, s32[1,2,2,4]{3,2,1,0:T(2,128)} %panel_fill_any.1, s32[1,2,16]{2,1,0:T(2,128)} %copy_fill_any.1, bf16[1,2,256,512]{3,2,1,0:T(8,128)(2,1)} %l_any.1, bf16[1,2,16,2048]{3,2,1,0:T(8,128)(2,1)} %u_any.1, bf16[15,256,256]{2,1,0:T(8,128)(2,1)} %sep_ref.1), custom_call_target="tpu_custom_call" | custom-call | flops 2147483648 | bytes 4194304 | tf_op jit(solution)/shard_map/pallas_call | solution.py:486
  85.8 1.6 %copy.8 = f32[256,128]{1,0:T(8,128)} copy(f32[256,128]{1,0:T(8,128)} %shard_map.64) | data formatting | bytes 262144

commit v5 on v4

--- a/solution.py
+++ b/solution.py
@@ -278,21 +278,17 @@
     late = []
 
     def each(low, act):
-        def body(d, carry):
+        for d in range(low, Z):
             act(d)
-            return carry
-
-        lax.fori_loop(low, Z, body, 0)
 
     def part_copies(level, cand, parts):
         return lambda d: remote(cand.at[along_z(d)], parts.at[d], part_sem, (level, d), to_z(d))
 
     def add_parts(own, parts, copies):
-        def add(d, total):
+        total = own.astype(F32)
+        for d in range(1, Z):
             copies(d).wait_recv()
-            return total + parts[d].astype(F32)
-
-        total = lax.fori_loop(1, Z, add, own.astype(F32))
+            total = total + parts[d].astype(F32)
         late.append((1, copies))
         return total
 

time: 87.6 us -> 87 us (level)
  no operation moved by 1% of the time
where the time goes in v5:
time: 87 us; the launch traced here: 86.8 us
  Pallas kernels  85.2 us (98%)
  local copies, waits for them, and re-layouts  1.57 us (2%)
    pallas_call x1, Pallas kernels, local(): pl.pallas_call(kernel, out_shape=jax.ShapeDtypeStruct((rows, BLOCK), F32)...  85.2 us

profile of v5, /device:TPU:56, one launch (start us, length us, event | category | flops | bytes accessed | tf_op | source)
XLA Modules:
  0.0 86.8 jit_solution(13139259054195229476)
XLA Ops:
  0.0 85.2 %shard_map.64 = f32[256,128]{1,0:T(8,128)} custom-call(s32[15]{0:T(128)} %owner_any.1, s32[1,2,2,4]{3,2,1,0:T(2,128)} %panel_fill_any.1, s32[1,2,16]{2,1,0:T(2,128)} %copy_fill_any.1, bf16[1,2,256,512]{3,2,1,0:T(8,128)(2,1)} %l_any.1, bf16[1,2,16,2048]{3,2,1,0:T(8,128)(2,1)} %u_any.1, bf16[15,256,256]{2,1,0:T(8,128)(2,1)} %sep_ref.1), custom_call_target="tpu_custom_call" | custom-call | flops 2147483648 | bytes 4194304 | tf_op jit(solution)/shard_map/pallas_call | solution.py:482
  85.3 1.6 %copy.8 = f32[256,128]{1,0:T(8,128)} copy(f32[256,128]{1,0:T(8,128)} %shard_map.64) | data formatting | bytes 262144

commit v6 on v5

--- a/solution.py
+++ b/solution.py
@@ -278,7 +278,7 @@
     late = []
 
     def each(low, act):
-        for d in range(low, Z):
+        for d in sorted(range(low, Z), key=lambda d: abs(d - Z // 2)):
             act(d)
 
     def part_copies(level, cand, parts):
@@ -299,8 +299,8 @@
         def there(d):
             return remote(theirs, pivot.at[1, z], pivot_sem, (level, Z + d), across(level + 1, d))
 
+        each(0, lambda d: there(d).start())
         each(1, lambda d: here(d).start())
-        each(0, lambda d: there(d).start())
         pivot[0, z] = mine[...]
         return here, there
 

time: 87 us -> 85.3 us (0.980)
  Pallas kernels: 85.2 us -> 83.6 us
    pallas_call x1, Pallas kernels: 85.2 us -> 83.6 us  [local(): pl.pallas_call(kernel, out_shape=jax.ShapeDtypeStruct((rows, BLOCK), F32)...]
where the time goes in v6:
time: 85.3 us; the launch traced here: 85.2 us
  Pallas kernels  83.6 us (98%)
  local copies, waits for them, and re-layouts  1.57 us (2%)
    pallas_call x1, Pallas kernels, local(): pl.pallas_call(kernel, out_shape=jax.ShapeDtypeStruct((rows, BLOCK), F32)...  83.6 us

profile of v6, /device:TPU:56, one launch (start us, length us, event | category | flops | bytes accessed | tf_op | source)
XLA Modules:
  0.0 85.2 jit_solution(12733731526867216715)
XLA Ops:
  0.0 83.6 %shard_map.64 = f32[256,128]{1,0:T(8,128)} custom-call(s32[15]{0:T(128)} %owner_any.1, s32[1,2,2,4]{3,2,1,0:T(2,128)} %panel_fill_any.1, s32[1,2,16]{2,1,0:T(2,128)} %copy_fill_any.1, bf16[1,2,256,512]{3,2,1,0:T(8,128)(2,1)} %l_any.1, bf16[1,2,16,2048]{3,2,1,0:T(8,128)(2,1)} %u_any.1, bf16[15,256,256]{2,1,0:T(8,128)(2,1)} %sep_ref.1), custom_call_target="tpu_custom_call" | custom-call | flops 2147483648 | bytes 4194304 | tf_op jit(solution)/shard_map/pallas_call | solution.py:482
  83.6 1.6 %copy.8 = f32[256,128]{1,0:T(8,128)} copy(f32[256,128]{1,0:T(8,128)} %shard_map.64) | data formatting | bytes 262144
